TPU v7x, 512 devices: a whole 4x4x16 slice. The times are simulated.
512 devices in a mesh: member: 64 (over z, x), region: 8 (over y, core).
Axes of the slice: x: 4, y: 4, z: 16, core: 2. Of those that a mesh axis runs over, the one named last changes fastest.
Arguments:
- states: bfloat16 [512, 1024, 768], P('member', 'region'), may hold values from -6 to 6
- observed: bfloat16 [512, 1024, 256], P('member', 'region'), may hold values from -6 to 6
- precision: float32 [1024, 256], P('region'), may hold values from 0.3 to 4
- innovation: float32 [1024, 256], P('region'), may hold values from -6 to 6
- obs_column: int32 [1024, 256], P('region'), may hold values from 0 to 63
- nearby: int32 [1024, 3], P('region'), may hold values from 0 to 1023, as said below
Outputs:
- analysis: bfloat16 [512, 1024, 768], P('member', 'region')
Inputs may be any that keep to these rules, and one draw needn't show every extreme that they name: `nearby`: row b lists 3 different observation blocks: b itself first, then blocks at cycle distance at most 4 from b (blocks 0 and 1024 - 1 are neighbours), one at distance exactly 4.
All inputs are finite; a program needn't handle non-finite values. Where the computation divides by a largest or mean magnitude, that divisor is 1e-20 or more.
Results may differ from a plain program's by a relative error of at most 0.0043.
The roundings to bfloat16 on the way count: a program that leaves them out, or rounds other values in their place, can miss the bound.
Values may be sent and summed in bfloat16 or wider, within the bound.
A program may use at most 64 MiB of HBM per device.

v0:
```python
import jax
import jax.numpy as jnp
from jax import lax
from jax.sharding import PartitionSpec as P

COLS = 64
RADIUS = 4
NS_STEPS = 3


def extended_2(cells, sides, width):
    for axis, dim in sides:
        count = lax.axis_size(axis)
        head = lax.slice_in_dim(cells, 0, width, axis=dim)
        tail = lax.slice_in_dim(cells, cells.shape[dim] - width, cells.shape[dim], axis=dim)
        cells = jnp.concatenate(
            [
                lax.ppermute(tail, axis, [(i, (i + 1) % count) for i in range(count)]),
                cells,
                lax.ppermute(head, axis, [((i + 1) % count, i) for i in range(count)]),
            ],
            axis=dim,
        )
    return cells


def highest(left, right):
    return jnp.dot(left, right, precision=lax.Precision.HIGHEST)


def transform(members, obs_rows, obs_precision, obs_innovation, obs_columns, offsets):
    ensemble = members.shape[0]
    member_float = members.astype(jnp.float32)
    mean_state = jnp.mean(member_float, axis=0)
    state_pert = (member_float - mean_state).astype(jnp.bfloat16)
    obs_float = obs_rows.astype(jnp.float32)
    obs_pert = (obs_float - jnp.mean(obs_float, axis=0)).astype(jnp.bfloat16)
    distance = COLS * offsets + obs_columns - 0.5 * (COLS - 1)
    local_weight = obs_precision * jnp.exp(-0.5 * jnp.square(distance / (0.5 * COLS * RADIUS)))
    weighted = (obs_pert.astype(jnp.float32) * local_weight).astype(jnp.bfloat16)
    product = lax.dot_general(
        weighted, obs_pert, (((1,), (1,)), ((), ())), preferred_element_type=jnp.float32
    )
    forcing = highest(weighted.astype(jnp.float32), obs_innovation)
    identity = jnp.eye(ensemble, dtype=jnp.float32)
    system = product + (ensemble - 1.0) * identity
    row_bound = jnp.max(jnp.sum(jnp.abs(system), axis=1))
    root_iterate = system / row_bound
    inverse_root = identity
    for iteration in range(NS_STEPS):
        if iteration == 0:
            factor = 1.5 * identity - 0.5 * root_iterate
        else:
            factor = 1.5 * identity - 0.5 * highest(inverse_root, root_iterate)
        if iteration < NS_STEPS - 1:
            root_iterate = highest(root_iterate, factor)
        inverse_root = factor if iteration == 0 else highest(factor, inverse_root)
    mean_weight = highest(inverse_root, highest(inverse_root, forcing)) / row_bound
    weights = (jnp.sqrt((ensemble - 1.0) / row_bound) * inverse_root + mean_weight[:, None]).astype(
        jnp.bfloat16
    )
    analysed = lax.dot_general(
        weights, state_pert, (((0,), (0,)), ((), ())), preferred_element_type=jnp.float32
    )
    return (mean_state + analysed).astype(jnp.bfloat16)


def on_device(states, observed, precision, innovation, obs_column, nearby):
    local_blocks = states.shape[1]
    member_count = lax.axis_size("member")
    per_device = local_blocks // member_count
    near_count = nearby.shape[1]
    obs_count = observed.shape[2]
    total_blocks = local_blocks * lax.axis_size("region")
    first_block = lax.axis_index("region") * local_blocks
    block_ids = first_block + jnp.arange(local_blocks, dtype=jnp.int32)
    offsets = (
        jnp.mod(nearby - block_ids[:, None] + total_blocks // 2, total_blocks) - total_blocks // 2
    )
    extended = extended_2(observed, (("region", 1),), RADIUS)
    obs_meta = jnp.stack([precision, innovation, obs_column.astype(jnp.float32)])
    meta_ext = extended_2(obs_meta, (("region", 1),), RADIUS)
    member_rank = lax.axis_index("member")
    own_offsets = lax.dynamic_slice_in_dim(offsets, member_rank * per_device, per_device, 0)
    own_blocks = member_rank * per_device + jnp.arange(per_device, dtype=jnp.int32)
    window_span = per_device + 2 * RADIUS
    picked_rows = (
        jnp.arange(member_count, dtype=jnp.int32)[:, None] * per_device
        + jnp.arange(window_span, dtype=jnp.int32)[None, :]
    ).reshape(-1)
    outgoing = jnp.take(extended, picked_rows, axis=1)
    gathered_states, arrived = (
        lax.all_to_all(states, "member", split_axis=1, concat_axis=0, tiled=True),
        lax.all_to_all(outgoing, "member", split_axis=1, concat_axis=0, tiled=True),
    )
    ensemble = gathered_states.shape[0]
    window_rows = (jnp.arange(per_device, dtype=jnp.int32)[:, None] + own_offsets + RADIUS).reshape(
        -1
    )
    arrived = jnp.take(arrived, window_rows, axis=1)
    obs_blocks = arrived.reshape(ensemble, per_device, near_count * obs_count)
    meta_rows = (own_blocks[:, None] + own_offsets + RADIUS).reshape(-1)
    own_meta = jnp.take(meta_ext, meta_rows, axis=1).reshape(3, per_device, near_count * obs_count)
    offset_float = jnp.repeat(own_offsets.astype(jnp.float32), obs_count, axis=1)
    analysed = jax.vmap(transform, in_axes=(1, 1, 0, 0, 0, 0), out_axes=1)(
        gathered_states, obs_blocks, own_meta[0], own_meta[1], own_meta[2], offset_float
    )
    return lax.all_to_all(analysed, "member", split_axis=0, concat_axis=1, tiled=True)


def solution(mesh):
    placed = (
        P("member", "region", None),
        P("member", "region", None),
        P("region", None),
        P("region", None),
        P("region", None),
        P("region", None),
    )
    return jax.shard_map(
        on_device,
        mesh=mesh,
        in_specs=placed,
        out_specs=P("member", "region", None),
        check_vma=False,
    )
```

profile of v0, /device:TPU:24, one launch (start us, length us, event | category | flops | bytes accessed | tf_op | source)
XLA Modules:
  0.0 364.2 jit_solution(17474475731766028308)
XLA Ops:
  0.0 3.4 copy.100
  3.4 18.7 %all-to-all-start = ((bf16[8,128,768]{2,0,1:T(8,128)(2,1)}), bf16[8,128,768]{2,0,1:T(8,128)(2,1)S(1)}, u32[]{:S(2)}, u32[]{:S(2)}) async-start(bf16[8,128,768]{2,0,1:T(8,128)(2,1)} %copy.100), calls=%async_computation | async-start | bytes 3145728 | tf_op jit(solution)/shard_map/all_to_all | solution.py:93
  22.1 0.3 copy.103
  22.5 1.7 collective-permute-start.1
  24.2 0.1 iota_add_fusion
  24.3 0.1 add.203
  24.4 0.1 add.200
  24.6 1.0 collective-permute-done
  25.6 0.0 collective-permute-done.1
  25.6 0.1 pad_maximum_fusion
  25.7 3.4 gather_fusion
  29.1 5.1 %select_bitcast_fusion = bf16[8,640,256]{2,0,1:T(8,128)(2,1)} fusion(bf16[640,8,256]{2,1,0:T(8,128)(2,1)} %gather_fusion, pred[640]{0:T(1024)(128)(4,1)S(1)} %compare_and_fusion), kind=kLoop, calls=%fused_computation.10 | loop fusion | flops 1310720 | bytes 5243520 | tf_op jit(solution)/shard_map/jit(_take)/select_n | solution.py:91
  34.2 65.7 %all-to-all-done = bf16[8,128,768]{2,0,1:T(8,128)(2,1)S(1)} async-done(((bf16[8,128,768]{2,0,1:T(8,128)(2,1)}), bf16[8,128,768]{2,0,1:T(8,128)(2,1)S(1)}, u32[]{:S(2)}, u32[]{:S(2)}) %all-to-all-start) | async-done | bytes 1572896 | tf_op jit(solution)/shard_map/all_to_all | solution.py:93
  99.9 6.1 %all-to-all-start.1 = ((bf16[8,640,256]{2,0,1:T(8,128)(2,1)}), bf16[8,640,256]{2,0,1:T(8,128)(2,1)}, u32[]{:S(2)}, u32[]{:S(2)}) async-start(bf16[8,640,256]{2,0,1:T(8,128)(2,1)} %select_bitcast_fusion), calls=%async_computation.1 | async-start | bytes 5242880 | tf_op jit(solution)/shard_map/all_to_all | solution.py:94
  106.0 0.1 stack.14
  106.1 0.1 stack.12
  106.2 0.1 stack.13
  106.4 1.7 collective-permute-start.3
  108.1 0.1 add_add_fusion
  108.2 0.1 copy.110
  108.3 0.1 reshape.206
  108.4 0.1 reshape.205
  108.5 0.1 convert_multiply_fusion
  108.5 0.1 copy.112
  108.6 0.1 copy.107
  108.7 0.1 reshape.204
  108.8 0.1 compare_and_fusion.2
  108.9 0.1 copy.102
  109.0 1.2 fusion.29
  110.2 1.1 fusion.28
  111.3 0.1 broadcast_bitcast_fusion.1
  111.4 0.1 broadcast_bitcast_fusion
  111.4 0.1 broadcast_in_dim.66
  111.6 0.4 pad_maximum_fusion.1
  111.9 0.6 gather_fusion.2
  112.5 0.1 select_bitcast_fusion.1
  112.7 1.0 convert_reduce_fusion.1
  113.7 0.2 reduce_sum.35
  114.0 0.2 reduce_sum.36
  114.1 1.9 convert_element_type.59
  116.0 112.0 %all-to-all-done.1 = bf16[8,640,256]{2,0,1:T(8,128)(2,1)} async-done(((bf16[8,640,256]{2,0,1:T(8,128)(2,1)}), bf16[8,640,256]{2,0,1:T(8,128)(2,1)}, u32[]{:S(2)}, u32[]{:S(2)}) %all-to-all-start.1) | async-done | bytes 2621472 | tf_op jit(solution)/shard_map/all_to_all | solution.py:94
  228.0 3.4 copy.163
  231.4 2.4 gather_fusion.1
  233.8 0.4 convert_reduce_fusion
  234.2 0.7 copy.108
  235.0 0.8 fusion.9
  235.7 0.4 copy-done.4
  236.2 2.6 abs_reduce_fusion
  238.8 0.1 reduce_max.9
  238.9 9.4 %fusion.8 = f32[2,512,512]{2,1,0:T(8,128)S(1)} fusion(f32[512,512]{0,1:T(8,128)S(1)} %copy-done, f32[2,512,512]{1,2,0:T(8,128)} %get-tuple-element.15, f32[2]{0:T(128)S(1)} %reduce_max.9, f32[512,512]{0,1:T(8,128)S(1)} %copy-done.5), kind=kOutput, calls=%fused_computation.21 | convolution fusion | flops 3224371200 | bytes 6291464 | tf_op jit(solution)/shard_map/vmap()/dot_general | solution.py:28
  248.3 4.5 %multiply_subtract_fusion = f32[2,512,512]{1,2,0:T(8,128)S(1)} fusion(f32[2,512,512]{2,1,0:T(8,128)S(1)} %fusion.8, f32[512,512]{0,1:T(8,128)S(1)} %copy-done, f32[2,512,512]{1,2,0:T(8,128)S(1)} %copy-done.11, f32[2]{0:T(128)S(1)} %reduce_max.9, f32[512,512]{0,1:T(8,128)S(1)} %copy-done.5), kind=kOutput, calls=%fused_computation.17 | convolution fusion | flops 3224371200 | bytes 8388616 | tf_op jit(solution)/shard_map/vmap()/dot_general | solution.py:28
  252.9 3.5 fusion.45
  256.4 7.1 %fusion.6 = f32[2,512,512]{2,1,0:T(8,128)S(1)} fusion(f32[2,512,512]{1,2,0:T(8,128)S(1)} %multiply_subtract_fusion, f32[512,512]{0,1:T(8,128)S(1)} %copy-done, f32[2,512,512]{1,2,0:T(8,128)S(1)} %copy-done.11, f32[2]{0:T(128)S(1)} %reduce_max.9, f32[512,512]{0,1:T(8,128)S(1)} %copy-done.5), kind=kOutput, calls=%fused_computation.19 | convolution fusion | flops 3223322624 | bytes 8388616 | tf_op jit(solution)/shard_map/vmap()/dot_general | solution.py:28
  263.6 4.0 %fusion.46 = f32[2,512,512]{1,2,0:T(8,128)S(1)} fusion(f32[2,512,512]{2,1,0:T(8,128)S(1)} %fusion.6, f32[2,512,512]{2,1,0:T(8,128)S(1)} %fusion.45), kind=kOutput, calls=%fused_computation.100 | convolution fusion | flops 3221225472 | bytes 6291456 | tf_op jit(solution)/shard_map/vmap()/dot_general | solution.py:28
  267.6 3.6 fusion.3
  271.2 0.9 fusion.1
  272.0 1.9 fusion.32
  273.9 1.9 fusion.30
  275.8 0.1 bitcast_divide_fusion
  275.9 1.2 fusion.15
  277.1 1.8 copy.126
  278.9 82.5 %all_to_all.45 = bf16[512,2,768]{2,1,0:T(2,128)(2,1)S(1)} all-to-all(bf16[512,2,768]{2,1,0:T(2,128)(2,1)S(1)} %copy.126), channel_id=1, replica_groups=mesh['member'=64,'region'=8] {'member'}, dimensions={0} | all-to-all | bytes 3145728 | tf_op jit(solution)/shard_map/all_to_all | solution.py:108
  361.4 1.1 copy.127
  362.5 1.5 all_to_all.41
  (54 shorter events, 0.3 us)
Async XLA Ops:
  3.4 18.7 %copy-start.6 = (bf16[8,128,256]{2,1,0:T(8,128)(2,1)S(1)}, bf16[8,128,256]{2,1,0:T(8,128)(2,1)}, u32[]{:S(2)}) copy-start(bf16[8,128,256]{2,1,0:T(8,128)(2,1)} %param.7) | copy-start | bytes 1572868
  3.4 96.5 %all-to-all-start = ((bf16[8,128,768]{2,0,1:T(8,128)(2,1)}), bf16[8,128,768]{2,0,1:T(8,128)(2,1)S(1)}, u32[]{:S(2)}, u32[]{:S(2)}) async-start(bf16[8,128,768]{2,0,1:T(8,128)(2,1)} %copy.100), calls=%async_computation | async-start | bytes 3145728 | tf_op jit(solution)/shard_map/all_to_all | solution.py:93
  22.4 3.2 collective-permute-start
  22.5 3.2 collective-permute-start.1
  34.2 71.8 %copy-start.7 = (s32[128,256]{1,0:T(8,128)S(1)}, s32[128,256]{1,0:T(8,128)}, u32[]{:S(2)}) copy-start(s32[128,256]{1,0:T(8,128)} %param.10) | copy-start | bytes 393220
  34.2 71.9 %copy-start.8 = (f32[128,256]{1,0:T(8,128)S(1)}, f32[128,256]{1,0:T(8,128)}, u32[]{:S(2)}) copy-start(f32[128,256]{1,0:T(8,128)} %param.8) | copy-start | bytes 393220
  34.2 72.0 %copy-start.9 = (f32[128,256]{1,0:T(8,128)S(1)}, f32[128,256]{1,0:T(8,128)}, u32[]{:S(2)}) copy-start(f32[128,256]{1,0:T(8,128)} %param.9) | copy-start | bytes 393220
  34.2 73.9 %copy-start.10 = (s32[128,3]{0,1:T(4,128)S(1)}, s32[128,3]{0,1:T(4,128)}, u32[]{:S(2)}) copy-start(s32[128,3]{0,1:T(4,128)} %param.11) | copy-start | bytes 4612
  99.9 128.1 %all-to-all-start.1 = ((bf16[8,640,256]{2,0,1:T(8,128)(2,1)}), bf16[8,640,256]{2,0,1:T(8,128)(2,1)}, u32[]{:S(2)}, u32[]{:S(2)}) async-start(bf16[8,640,256]{2,0,1:T(8,128)(2,1)} %select_bitcast_fusion), calls=%async_computation.1 | async-start | bytes 5242880 | tf_op jit(solution)/shard_map/all_to_all | solution.py:94
  106.3 5.2 %collective-permute-start.2 = (f32[3,4,256]{2,0,1:T(4,128)S(1)}, f32[3,4,256]{2,0,1:T(4,128)S(1)}, u32[]{:S(2)}, u32[]{:S(2)}) collective-permute-start(f32[3,4,256]{2,0,1:T(4,128)S(1)} %get-tuple-element.9), channel_id=1, source_target_pairs={{0,1},{1,2},{2,3},{3,4},{4,5},{5,6},{6,7},{7,0},{8,9},{9,10},{10,1... | collective-permute-start | bytes 36872 | tf_op jit(solution)/shard_map/ppermute | solution.py:18
  106.4 5.2 %collective-permute-start.3 = (f32[3,4,256]{2,0,1:T(4,128)S(1)}, f32[3,4,256]{2,0,1:T(4,128)S(1)}, u32[]{:S(2)}, u32[]{:S(2)}) collective-permute-start(f32[3,4,256]{2,0,1:T(4,128)S(1)} %get-tuple-element.10), channel_id=1, source_target_pairs={{1,0},{2,1},{3,2},{4,3},{5,4},{6,5},{7,6},{0,7},{9,8},{10,9},{11,1... | collective-permute-start | bytes 36872 | tf_op jit(solution)/shard_map/ppermute | solution.py:20
  234.9 1.2 copy-start.4
  236.2 2.6 copy-start.2
  236.2 2.7 copy-start
  236.2 2.7 copy-start.5
  238.9 9.4 %copy-start.11 = (f32[2,512,512]{1,2,0:T(8,128)S(1)}, f32[2,512,512]{1,2,0:T(8,128)}, u32[]{:S(2)}) copy-start(f32[2,512,512]{1,2,0:T(8,128)} %get-tuple-element.15) | copy-start | bytes 6291460
  267.6 3.6 copy-start.3
  272.0 3.8 %copy-start.1 = (f32[8,128,768]{2,0,1:T(8,128)S(1)}, f32[8,128,768]{2,0,1:T(8,128)}, u32[]{:S(2)}) copy-start(f32[8,128,768]{2,0,1:T(8,128)} %convert_element_type.59) | copy-start | bytes 9437188
where the time goes:
time: 371 us; the launch traced here: 364 us
  waiting for transfers between devices  179 us (48%)
  blocking collectives  82.5 us (22%)
  matrix products  40.6 us (11%)
  starting transfers between devices  28.3 us (8%)
  local copies, waits for them, and re-layouts  20.8 us (6%)
  other arithmetic  12.7 us (3%)
    all_to_all x1, waiting for transfers between devices, on_device(): lax.all_to_all(outgoing, 'member', split_axis=1, concat_axis=0, tiled=True)  112 us
    all_to_all x1, blocking collectives, on_device(): lax.all_to_all(analysed, 'member', split_axis=0, concat_axis=1, tiled=True)  82.5 us
    all_to_all x1, waiting for transfers between devices, on_device(): lax.all_to_all(states, 'member', split_axis=1, concat_axis=0, tiled=True)  65.7 us
    dot_general x9, matrix products, highest(): return jnp.dot(left, right, precision=lax.Precision.HIGHEST)  36.8 us
    all_to_all x1, starting transfers between devices, on_device(): lax.all_to_all(states, 'member', split_axis=1, concat_axis=0, tiled=True)  18.7 us
  transfers between devices with their start and end apart: 6, of which 3 were waited for; matrix products, arithmetic and copies ran while one was open for 5% of the time, Pallas kernels for 0%

commit v1 on v0

v1 whole, which is shorter than its diff:
```python
import jax
import jax.numpy as jnp
from jax import lax
from jax.experimental import pallas as pl
from jax.experimental.pallas import tpu as pltpu
from jax.sharding import PartitionSpec as P

MESH = pl.DeviceIdType.MESH
F32 = jnp.float32
BF16 = jnp.bfloat16

COLS = 64
RADIUS = 4
NZ, NX, NY = 16, 4, 4
K = 512
OBS = 256
SITES = 768
WINDOW = 10
PIECES = 3
WIDTH = SITES // PIECES
HALF = K // 2


def dot_nn(a, b):
    return jnp.dot(a, b, preferred_element_type=F32)


def dot_nt(a, b):
    return lax.dot_general(a, b, (((1,), (1,)), ((), ())), preferred_element_type=F32)


def split_rows(v):
    high = v.astype(BF16).astype(F32)
    rest = v - high
    mid = rest.astype(BF16).astype(F32)
    low = rest - mid
    row = lax.broadcasted_iota(jnp.int32, (16, v.shape[1]), 0)
    zero = jnp.zeros((16, v.shape[1]), F32)
    stacked = jnp.where(row == 0, high, jnp.where(row == 1, mid, jnp.where(row == 2, low, zero)))
    return stacked.astype(BF16)


def as_row(v):
    return jnp.concatenate([v[0:1], v[1:2]], axis=1)


def identity_rows(start, scale):
    row = lax.broadcasted_iota(jnp.int32, (HALF, K), 0) + start
    col = lax.broadcasted_iota(jnp.int32, (HALF, K), 1)
    return jnp.where(row == col, F32(scale), F32(0.0))


def kernel(
    states, obs, meta, out,
    own_obs, window, arrived, results, meta_win, pert, weighted, innov, high, low, full, trans,
    meta_send, meta_recv, obs_send, obs_recv, win_send, win_recv, st_send, st_recv, out_send, out_recv,
):
    member = lax.axis_index("member")
    region = lax.axis_index("region")
    z, x = lax.div(member, NX), lax.rem(member, NX)
    y, c = lax.div(region, 2), lax.rem(region, 2)
    half, inner = lax.div(z, 8), lax.rem(z, 8)
    place = 2 * x + c
    z_next, z_prev = lax.rem(z + 1, NZ), lax.rem(z + NZ - 1, NZ)
    y_next = lax.rem(y + lax.div(z + 1, NZ), NY)
    y_prev = lax.rem(y + NY - 1 + lax.div(z + NZ - 1, NZ), NY)
    holder = c == half

    def device(zz, xx, yy, cc):
        return (zz * NX + xx, yy * 2 + cc)

    def remote(src, dst, send, recv, target):
        pltpu.make_async_remote_copy(
            src_ref=src, dst_ref=dst, send_sem=send, recv_sem=recv, device_id=target, device_id_type=MESH
        ).start()

    def local(src, dst, sem):
        pltpu.make_async_copy(src, dst, sem).start()

    def drain(ref, sem):
        pltpu.make_async_copy(ref, ref, sem).wait()

    def slot_of(zz, xx):
        return xx * 16 + lax.rem(zz, 2) * 8 + lax.div(zz, 2)

    barrier = pltpu.get_barrier_semaphore()

    def greet(t, carry):
        target = device(
            lax.rem(z + lax.div(t, 8), NZ), lax.rem(x + lax.rem(lax.div(t, 2), NX), NX), y, lax.rem(c + t, 2)
        )
        pl.semaphore_signal(barrier, inc=1, device_id=target, device_id_type=MESH)
        return carry

    lax.fori_loop(1, NZ * NX * 2, greet, 0)
    edge = (z == 0) | (z == NZ - 1)

    @pl.when(edge)
    def _():
        zz = NZ - 1 - z
        yy = lax.select(z == 0, y_prev, y_next)
        for j in range(8):
            pl.semaphore_signal(barrier, inc=1, device_id=device(zz, j // 2, yy, j % 2), device_id_type=MESH)

    pl.semaphore_wait(barrier, NZ * NX * 2 - 1 + 8 * edge.astype(jnp.int32))

    parity = lax.rem(z, 2)

    def send_obs(t, carry):
        ii = lax.rem(inner + t, 8)
        zz = 8 * c + ii
        src = obs.at[pl.ds(pl.multiple_of(ii * 128, 128), 128)]
        dst = own_obs.at[lax.div(z, 2)]
        mine = (zz == z) & (parity == c)

        @pl.when(mine)
        def _():
            local(src, dst, obs_recv)

        @pl.when(jnp.logical_not(mine))
        def _():
            remote(src, dst, obs_send, obs_recv, device(zz, x, y, parity))

        return carry

    lax.fori_loop(0, 8, send_obs, 0)

    @pl.when(holder)
    def _():
        start = inner * 16
        own = meta.at[pl.ds(start, 16)]
        local(own, meta_win.at[pl.ds(8, 16)], meta_recv)
        remote(own, meta_win.at[pl.ds(8, 16)], meta_send, meta_recv, device(z, x, y, 1 - c))
        for cc in range(2):
            remote(meta.at[pl.ds(start, 8)], meta_win.at[pl.ds(24, 8)], meta_send, meta_recv,
                   device(z_prev, x, y_prev, cc))
            remote(meta.at[pl.ds(start + 8, 8)], meta_win.at[pl.ds(0, 8)], meta_send, meta_recv,
                   device(z_next, x, y_next, cc))

    def send_states(piece):
        cols = pl.ds(piece * WIDTH, WIDTH)

        def body(t, carry):
            ii = lax.rem(inner + lax.div(t, 8), 8)
            zz = 8 * c + ii
            xx = lax.rem(x + lax.rem(lax.div(t, 2), NX), NX)
            cc = lax.rem(c + t, 2)
            src = states.at[ii * 8 + 2 * xx + cc, :, cols]
            dst = arrived.at[slot_of(z, x), :, cols]
            mine = (zz == z) & (xx == x) & (cc == c)

            @pl.when(mine)
            def _():
                local(src, dst, st_recv.at[piece])

            @pl.when(jnp.logical_not(mine))
            def _():
                remote(src, dst, st_send, st_recv.at[piece], device(zz, xx, y, cc))

            return carry

        lax.fori_loop(0, 64, body, 0)

    self_obs = holder & (parity == c)

    @pl.when(self_obs)
    def _():
        drain(own_obs.at[pl.ds(0, 7)], obs_send)

    @pl.when(jnp.logical_not(self_obs))
    def _():
        drain(own_obs, obs_send)

    send_states(0)
    drain(own_obs, obs_recv)

    mine_at = pl.ds(pl.multiple_of(place * 8, 8), 8)
    for step in range(8):
        for q in range(8):
            first, last = max(0, 2 * q - 4), min(16, 2 * q + 6)
            src = own_obs.at[:, pl.ds(first * 8, (last - first) * 8)]
            dst = window.at[mine_at, pl.ds((first - 2 * q + 4) * 8, (last - first) * 8)]
            if step > 0:

                @pl.when(lax.rem(place + step, 8) == q)
                def _():
                    remote(src, dst, win_send, win_recv, device(z, q // 2, y, q % 2))

            else:

                @pl.when(place == q)
                def _():
                    local(src, dst, win_recv)

    for q, rows in ((0, 4), (1, 2)):
        remote(own_obs.at[:, pl.ds((16 - rows) * 8, rows * 8)], window.at[mine_at, pl.ds(0, rows * 8)],
               win_send, win_recv, device(z_next, q // 2, y_next, q % 2))
    for q, rows in ((7, 4), (6, 2)):
        remote(own_obs.at[:, pl.ds(0, rows * 8)], window.at[mine_at, pl.ds((WINDOW - rows) * 8, rows * 8)],
               win_send, win_recv, device(z_prev, q // 2, y_prev, q % 2))

    for piece in range(1, PIECES):
        send_states(piece)

    drain(meta_win, meta_recv)
    listed = [meta_win[8 + 2 * place + b][6:7] for b in range(2)]
    local_weight = [[None] * WINDOW for _ in range(2)]
    for w in range(WINDOW):
        row = meta_win[2 * place + 4 + w]
        precision, column = row[0:2], row[4:6]
        innov[:, w * OBS : (w + 1) * OBS] = split_rows(as_row(row[2:4]))
        for b in range(2):
            if 0 <= w - b <= 2 * RADIUS:
                distance = F32(COLS * (w - b - RADIUS)) + column - F32(0.5 * (COLS - 1))
                decay = jnp.exp(-0.5 * jnp.square(distance / (0.5 * COLS * RADIUS)))
                local_weight[b][w] = as_row(precision * decay * listed[b][:, w - b : w - b + 1])

    drain(window, win_recv)
    for pair in range(WINDOW // 2):
        rows = window[:, pair * 16 : (pair + 1) * 16, :].astype(F32)
        for e in range(2):
            w = 2 * pair + e
            at = slice(w * OBS, (w + 1) * OBS)
            values = rows[:, 8 * e : 8 * e + 8, :].reshape(K, OBS)
            anomaly = (values - jnp.mean(values, axis=0, keepdims=True)).astype(BF16)
            pert[:, at] = anomaly
            anomaly = anomaly.astype(F32)
            for b in range(2):
                if local_weight[b][w] is not None:
                    weighted[b, :, at] = (anomaly * local_weight[b][w]).astype(BF16)

    def put(k, rows, value):
        top = value.astype(BF16)
        high[k, rows, :] = top
        low[k, rows, :] = (value - top.astype(F32)).astype(BF16)

    def product(a, b, rows):
        left = high[a, rows, :]
        return dot_nn(left, high[b]) + dot_nn(left, low[b]) + dot_nn(low[a, rows, :], high[b])

    def halves(step):
        @pl.loop(0, 2)
        def _(t):
            start = pl.multiple_of(t * HALF, HALF)
            step(pl.ds(start, HALF), start)

    def times(v, k):
        parts = split_rows(v)
        return jnp.sum(dot_nn(parts, high[k]) + dot_nn(parts, low[k]), axis=0, keepdims=True)

    R, F0, R1, F1, R2, Z2, F2, Z3 = range(8)

    @pl.loop(0, 2)
    def _(b):
        span = pl.ds(pl.multiple_of(b * OBS, OBS), (2 * RADIUS + 1) * OBS)

        def system(rows, start):
            full[rows, :] = dot_nt(pert[rows, span], weighted[b, :, span]) + identity_rows(start, K - 1.0)

        halves(system)
        row_bound = jnp.max(jnp.sum(jnp.abs(full[...]), axis=0, keepdims=True), axis=1, keepdims=True)
        inverse = 1.0 / row_bound

        def first(rows, start):
            value = full[rows, :] * inverse
            put(R, rows, value)
            put(F0, rows, identity_rows(start, 1.5) - 0.5 * value)

        def second(rows, start):
            put(R1, rows, product(R, F0, rows))

        def third(rows, start):
            put(F1, rows, identity_rows(start, 1.5) - 0.5 * product(F0, R1, rows))

        def fourth(rows, start):
            put(R2, rows, product(R1, F1, rows))
            put(Z2, rows, product(F1, F0, rows))

        def fifth(rows, start):
            put(F2, rows, identity_rows(start, 1.5) - 0.5 * product(Z2, R2, rows))

        def sixth(rows, start):
            value = product(F2, Z2, rows)
            full[rows, :] = value
            put(Z3, rows, value)

        for step in (first, second, third, fourth, fifth, sixth):
            halves(step)

        forcing = jnp.sum(dot_nt(innov[:, span], weighted[b, :, span]), axis=0, keepdims=True)
        mean_weight = times(times(forcing, Z3), Z3) * inverse
        scale = jnp.sqrt((K - 1.0) * inverse)

        def weights(rows, start):
            trans[b, rows, :] = (scale * full[rows, :] + mean_weight).astype(BF16)

        halves(weights)

    for piece in range(PIECES):
        cols = pl.ds(piece * WIDTH, WIDTH)
        drain(arrived.at[:, :, cols], st_recv.at[piece])
        chunk = arrived[:, :, piece * WIDTH : (piece + 1) * WIDTH].astype(F32)
        blocks = []
        for b in range(2):
            values = chunk[:, 8 * b : 8 * b + 8, :].reshape(K, WIDTH)
            mean = jnp.mean(values, axis=0, keepdims=True)
            analysed = mean + dot_nn(trans[b], (values - mean).astype(BF16))
            blocks.append(analysed.reshape(64, 8, WIDTH))
        results[:, :, piece * WIDTH : (piece + 1) * WIDTH] = jnp.concatenate(blocks, axis=1).astype(BF16)

        def give_back(t, carry):
            zz = lax.rem(z + lax.div(t, NX), NZ)
            xx = lax.rem(x + t, NX)
            src = results.at[slot_of(zz, xx), :, cols]
            dst = out.at[inner * 8 + place, :, cols]
            mine = (zz == z) & (xx == x) & holder

            @pl.when(mine)
            def _():
                local(src, dst, out_recv)

            @pl.when(jnp.logical_not(mine))
            def _():
                remote(src, dst, out_send, out_recv, device(zz, xx, y, half))

            return carry

        lax.fori_loop(0, 64, give_back, 0)

    drain(out, out_recv)

    @pl.when(holder)
    def _():
        drain(meta.at[pl.ds(0, 48)], meta_send)
        drain(states.at[pl.ds(0, 63)], st_send)
        drain(results.at[pl.ds(0, 63)], out_send)

    @pl.when(jnp.logical_not(holder))
    def _():
        drain(states, st_send)
        drain(results, out_send)

    for q in range(8):
        kept = min(16, 2 * q + 6) - max(0, 2 * q - 4)

        @pl.when(place == q)
        def _():
            drain(own_obs.at[:, pl.ds(0, (16 - kept) * 8)], win_send)

    for _ in range(4):
        drain(own_obs, win_send)


def on_device(states, observed, precision, innovation, obs_column, nearby):
    local_blocks = states.shape[1]
    total_blocks = local_blocks * lax.axis_size("region")
    block_ids = lax.axis_index("region") * local_blocks + jnp.arange(local_blocks, dtype=jnp.int32)
    offsets = (
        jnp.mod(nearby - block_ids[:, None] + total_blocks // 2, total_blocks) - total_blocks // 2
    )
    lanes = jnp.arange(128, dtype=jnp.int32) - RADIUS
    listed = jnp.any(offsets[:, :, None] == lanes[None, None, :], axis=1).astype(F32)
    meta = jnp.concatenate(
        [precision, innovation, obs_column.astype(F32), listed, jnp.zeros_like(listed)], axis=1
    ).reshape(local_blocks, 8, 128)
    chunks = states.reshape(8, 64, 2, SITES).transpose(1, 2, 0, 3).reshape(64, 16, SITES)
    obs_rows = observed.transpose(1, 0, 2).reshape(local_blocks * 8, OBS)

    vmem = pl.BlockSpec(memory_space=pltpu.VMEM)
    dma = pltpu.SemaphoreType.DMA
    gathered = pl.pallas_call(
        kernel,
        out_shape=jax.ShapeDtypeStruct((64, 16, SITES), BF16),
        in_specs=[vmem] * 3,
        out_specs=vmem,
        scratch_shapes=[
            pltpu.VMEM((8, 128, OBS), BF16),
            pltpu.VMEM((64, 8 * WINDOW, OBS), BF16),
            pltpu.VMEM((64, 16, SITES), BF16),
            pltpu.VMEM((64, 16, SITES), BF16),
            pltpu.VMEM((32, 8, 128), F32),
            pltpu.VMEM((K, WINDOW * OBS), BF16),
            pltpu.VMEM((2, K, WINDOW * OBS), BF16),
            pltpu.VMEM((16, WINDOW * OBS), BF16),
            pltpu.VMEM((8, K, K), BF16),
            pltpu.VMEM((8, K, K), BF16),
            pltpu.VMEM((K, K), F32),
            pltpu.VMEM((2, K, K), BF16),
            dma, dma, dma, dma, dma, dma, dma, dma((PIECES,)), dma, dma,
        ],
        compiler_params=pltpu.CompilerParams(
            collective_id=0, has_side_effects=True, vmem_limit_bytes=48 * 1024 * 1024
        ),
    )(chunks, obs_rows, meta)
    return gathered.reshape(64, 2, 8, SITES).transpose(2, 0, 1, 3).reshape(8, local_blocks, SITES)


def solution(mesh):
    split = P("region", None)
    placed = (P("member", "region", None), P("member", "region", None), split, split, split, split)
    return jax.shard_map(
        on_device, mesh=mesh, in_specs=placed, out_specs=P("member", "region", None), check_vma=False
    )
```

time: 371 us -> 197 us (0.53)
  the two profiles are of different devices: /device:TPU:24 before, /device:TPU:1 now
where the time goes in v1:
time: 197 us
  Pallas kernels  190 us (96%)
  local copies, waits for them, and re-layouts  5.58 us (3%)
    pallas_call x1, Pallas kernels, on_device(): pl.pallas_call(kernel, out_shape=jax.ShapeDtypeStruct((64, 16, SITES), BF...  190 us

profile of v1, /device:TPU:1, one launch (start us, length us, event | category | flops | bytes accessed | tf_op | source)
XLA Modules:
  0.0 196.7 jit_solution(17848469356160471104)
XLA Ops:
  0.0 0.0 copy-start.1
  0.0 0.0 copy-start
  0.0 0.8 fusion.1
  0.8 0.1 compare_reduce_fusion
  1.0 1.3 copy.18
  2.3 0.9 constant_dynamic-update-slice_fusion.1
  3.2 0.9 constant_dynamic-update-slice_fusion
  4.1 0.0 copy-done.1
  4.2 0.1 copy.16
  4.3 0.0 copy-done
  4.3 0.9 copy.14
  5.2 190.1 %shard_map.64 = bf16[64,16,768]{2,1,0:T(8,128)(2,1)S(1)} custom-call(bf16[64,16,768]{2,1,0:T(8,128)(2,1)S(1)} %bitcast.17, bf16[1024,256]{1,0:T(8,128)(2,1)S(1)} %bitcast.18, f32[128,8,128]{2,1,0:T(8,128)S(1)} %bitcast.19), custom_call_target="tpu_custom_call" | custom-call | tf_op jit(solution)/shard_map/pallas_call | solution.py:371
  195.3 1.4 copy.15
  (5 shorter events, 0.0 us)
Async XLA Ops:
  0.0 4.1 %copy-start.1 = (s32[128,256]{1,0:T(8,128)S(1)}, s32[128,256]{1,0:T(8,128)}, u32[]{:S(2)}) copy-start(s32[128,256]{1,0:T(8,128)} %param.10) | copy-start | bytes 393220
  0.0 4.3 %copy-start = (bf16[8,128,768]{2,1,0:T(8,128)(2,1)S(1)}, bf16[8,128,768]{2,1,0:T(8,128)(2,1)}, u32[]{:S(2)}) copy-start(bf16[8,128,768]{2,1,0:T(8,128)(2,1)} %param.6) | copy-start | bytes 4718596

commit v2 on v1

v2 whole, which is shorter than its diff:
```python
import jax
import jax.numpy as jnp
from jax import lax
from jax.experimental import pallas as pl
from jax.experimental.pallas import tpu as pltpu
from jax.sharding import PartitionSpec as P

MESH = pl.DeviceIdType.MESH
F32 = jnp.float32
BF16 = jnp.bfloat16

COLS = 64
RADIUS = 4
NBLK = 1024
NZ, NX, NY = 16, 4, 4
K = 512
OBS = 256
SITES = 768
PAIRS = 5
PIECES = 3
WIDTH = SITES // PIECES
TILE = 256


def dot_nn(a, b):
    return jnp.dot(a, b, preferred_element_type=F32)


def dot_nt(a, b):
    return lax.dot_general(a, b, (((1,), (1,)), ((), ())), preferred_element_type=F32)


def split_rows(v):
    top = v.astype(BF16).astype(F32)
    rest = v - top
    mid = rest.astype(BF16).astype(F32)
    row = lax.broadcasted_iota(jnp.int32, (16, v.shape[1]), 0)
    zero = jnp.zeros((16, v.shape[1]), F32)
    stacked = jnp.where(row == 0, top, jnp.where(row == 1, mid, jnp.where(row == 2, rest - mid, zero)))
    return stacked.astype(BF16)


def as_row(v):
    return jnp.concatenate([v[0:1], v[1:2]], axis=1)


def identity_rows(start, scale):
    row = lax.broadcasted_iota(jnp.int32, (TILE, K), 0) + start
    col = lax.broadcasted_iota(jnp.int32, (TILE, K), 1)
    return jnp.where(row == col, F32(scale), F32(0.0))


def kernel(
    states_hbm, observed_hbm, precision_hbm, innovation_hbm, column_hbm, nearby_hbm, out,
    states, observed, precision, innovation, column, nearby, load_sem,
    wide, chunks, obs, meta, own_obs, window, arrived, results, meta_win, weighted, high, low, full, trans,
    meta_send, meta_recv, obs_send, obs_recv, win_send, win_recv, st_send, st_recv, out_send, out_recv,
    row_ready,
):
    member = lax.axis_index("member")
    region = lax.axis_index("region")
    z, x = lax.div(member, NX), lax.rem(member, NX)
    y, c = lax.div(region, 2), lax.rem(region, 2)
    half, inner = lax.div(z, 8), lax.rem(z, 8)
    place = 2 * x + c
    parity = lax.rem(z, 2)
    z_next, z_prev = lax.rem(z + 1, NZ), lax.rem(z + NZ - 1, NZ)
    y_next = lax.rem(y + lax.div(z + 1, NZ), NY)
    y_prev = lax.rem(y + NY - 1 + lax.div(z + NZ - 1, NZ), NY)
    holder = c == half

    def device(zz, xx, yy, cc):
        return (zz * NX + xx, yy * 2 + cc)

    def remote(src, dst, send, recv, target):
        pltpu.make_async_remote_copy(
            src_ref=src, dst_ref=dst, send_sem=send, recv_sem=recv, device_id=target, device_id_type=MESH
        ).start()

    def pass_on(src, dst, send, recv, target, mine):
        @pl.when(mine)
        def _():
            pltpu.make_async_copy(src, dst, recv).start()

        @pl.when(jnp.logical_not(mine))
        def _():
            remote(src, dst, send, recv, target)

    def drain(ref, sem):
        pltpu.make_async_copy(ref, ref, sem).wait()

    def slot_of(zz, xx):
        return xx * 16 + lax.rem(zz, 2) * 8 + lax.div(zz, 2)

    loads = [
        pltpu.make_async_copy(source, target, load_sem.at[k])
        for k, (source, target) in enumerate((
            (observed_hbm, observed), (states_hbm, states), (precision_hbm, precision),
            (innovation_hbm, innovation), (column_hbm, column), (nearby_hbm, nearby),
        ))
    ]
    for load in loads:
        load.start()

    barrier = pltpu.get_barrier_semaphore()

    def greet(semaphore, zz, xx, yy, cc):
        @pl.when((zz != z) | (xx != x) | (yy != y) | (cc != c))
        def _():
            pl.semaphore_signal(semaphore, inc=1, device_id=device(zz, xx, yy, cc), device_id_type=MESH)

    for j in range(8):
        greet(barrier, 2 * j + c, x, y, half)
        greet(barrier, 8 * c + j, x, y, parity)
        greet(barrier, z, j // 2, y, j % 2)
        greet(barrier, z_next, j // 2, y_next, j % 2)
        greet(barrier, z_prev, j // 2, y_prev, j % 2)
    self_obs = holder & (parity == c)
    def by_block(source, target):
        for j in range(source.shape[2] // 128):
            lanes = slice(128 * j, 128 * j + 128)
            for k in range(8):
                wide[pl.ds(1024 * j + k, 128, stride=8), :] = source[k, :, lanes].astype(F32)
            target[..., lanes] = wide[1024 * j : 1024 * j + 1024, :].astype(BF16).reshape(target.shape[:-1] + (128,))

    loads[0].wait()
    by_block(observed, obs)
    pl.semaphore_wait(barrier, 39 - 2 * self_obs.astype(jnp.int32))

    for j in range(8):
        greet(row_ready, 2 * j + c, x, y, half)

    def send_obs(t, carry):
        ii = lax.rem(inner + t, 8)
        zz = 8 * c + ii
        src = obs.at[pl.ds(pl.multiple_of(ii * 128, 128), 128)]
        pass_on(src, own_obs.at[lax.div(z, 2)], obs_send, obs_recv, device(zz, x, y, parity),
                (zz == z) & (parity == c))
        return carry

    lax.fori_loop(0, 8, send_obs, 0)

    loads[1].wait()
    by_block(states, chunks)

    def send_states(piece, turns, per_z):
        cols = pl.ds(piece * WIDTH, WIDTH)

        def body(t, carry):
            zz = 8 * c + lax.rem(inner + lax.div(t, per_z), 8)
            turn = turns + lax.rem(t, per_z)
            xx = lax.rem(x + lax.div(turn, 2), NX)
            cc = lax.rem(c + turn, 2)
            src = chunks.at[lax.rem(zz, 8) * 8 + 2 * xx + cc, :, cols]
            pass_on(src, arrived.at[slot_of(z, x), :, cols], st_send, st_recv.at[piece], device(zz, xx, y, cc),
                    (zz == z) & (xx == x) & (cc == c))
            return carry

        lax.fori_loop(0, 8 * per_z, body, 0)

    pl.semaphore_wait(row_ready, 8 - self_obs.astype(jnp.int32))
    for piece in range(PIECES):
        send_states(piece, 0, 2)

    for load in loads[2:]:
        load.wait()
    for j in range(2):
        lanes = slice(128 * j, 128 * j + 128)
        meta[pl.ds(j, 128, stride=8), :] = precision[:, lanes]
        meta[pl.ds(2 + j, 128, stride=8), :] = innovation[:, lanes]
        meta[pl.ds(4 + j, 128, stride=8), :] = column[:, lanes].astype(F32)
    block = region * 128 + lax.broadcasted_iota(jnp.int32, (128, 128), 1)
    reach = lax.broadcasted_iota(jnp.int32, (128, 128), 0) - RADIUS
    listed = jnp.zeros((128, 128), F32)
    for q in range(3):
        offset = ((nearby[q : q + 1, :] - block + NBLK // 2) & (NBLK - 1)) - NBLK // 2
        listed = jnp.where(offset == reach, F32(1.0), listed)
    listed = listed.T
    meta[pl.ds(6, 128, stride=8), :] = listed
    meta[pl.ds(7, 128, stride=8), :] = jnp.zeros((128, 128), F32)

    @pl.when(holder)
    def _():
        start = pl.multiple_of(inner * 128, 128)
        own = meta.at[pl.ds(start, 128)]
        pltpu.make_async_copy(own, meta_win.at[pl.ds(64, 128)], meta_recv).start()
        remote(own, meta_win.at[pl.ds(64, 128)], meta_send, meta_recv, device(z, x, y, 1 - c))
        for cc in range(2):
            remote(meta.at[pl.ds(start, 64)], meta_win.at[pl.ds(192, 64)], meta_send, meta_recv,
                   device(z_prev, x, y_prev, cc))
            remote(meta.at[pl.ds(start + 64, 64)], meta_win.at[pl.ds(0, 64)], meta_send, meta_recv,
                   device(z_next, x, y_next, cc))

    @pl.when(self_obs)
    def _():
        drain(own_obs.at[pl.ds(0, 7)], obs_send)

    @pl.when(jnp.logical_not(self_obs))
    def _():
        drain(own_obs, obs_send)

    drain(own_obs, obs_recv)

    mine_at = pl.ds(pl.multiple_of(place * 8, 8), 8)
    for t in range(PAIRS):

        def send_pair(step, carry):
            u = lax.rem(place + step, 8)
            q = u + 2 - t
            target = device(
                lax.select(q < 0, z_prev, lax.select(q > 7, z_next, z)),
                lax.rem(lax.div(q + 8, 2), NX),
                lax.select(q < 0, y_prev, lax.select(q > 7, y_next, y)),
                lax.rem(q + 8, 2),
            )
            pass_on(own_obs.at[:, pl.ds(pl.multiple_of(u * 16, 16), 16)], window.at[t, mine_at],
                    win_send, win_recv.at[t], target, q == place)
            return carry

        lax.fori_loop(0, 8, send_pair, 0)

    for piece in range(PIECES):
        send_states(piece, 2, 6)
    drain(meta_win, meta_recv)

    def meta_of(row):
        return meta_win[pl.ds(pl.multiple_of(row * 8, 8), 8), :]

    listed_by = [meta_of(8 + 2 * place + b)[6:7] for b in range(2)]
    forcing = [jnp.zeros((16, K), F32) for _ in range(2)]
    for t in range(PAIRS):
        drain(window.at[t], win_recv.at[t])
        rows = window[t].astype(F32)
        perts, innov = [], []
        for e in range(2):
            w = 2 * t + e
            about = meta_of(2 * place + 4 + w)
            innov.append(split_rows(as_row(about[2:4])))
            values = rows[:, 8 * e : 8 * e + 8, :].reshape(K, OBS)
            pert = (values - jnp.mean(values, axis=0, keepdims=True)).astype(BF16)
            perts.append(pert)
            for b in range(2):
                if 0 <= w - b <= 2 * RADIUS:
                    distance = F32(COLS * (w - b - RADIUS)) + about[4:6] - F32(0.5 * (COLS - 1))
                    decay = jnp.exp(-0.5 * jnp.square(distance / (0.5 * COLS * RADIUS)))
                    local = as_row(about[0:2] * decay * listed_by[b][:, w - b : w - b + 1])
                    weighted[b, e] = (pert.astype(F32) * local).astype(BF16)
        for b in range(2):
            for e in range(2):
                w = 2 * t + e
                if 0 <= w - b <= 2 * RADIUS:
                    term = dot_nt(perts[e], weighted[b, e])
                    full[b] = term if w == b else full[b] + term
                    forcing[b] = forcing[b] + dot_nt(innov[e], weighted[b, e])

    def put(b, k, rows, value):
        top = value.astype(BF16)
        high[b, k, rows, :] = top
        low[b, k, rows, :] = (value - top.astype(F32)).astype(BF16)

    def held(b, k, rows):
        return high[b, k, rows, :].astype(F32) + low[b, k, rows, :].astype(F32)

    def product(b, i, j, rows):
        left = high[b, i, rows, :]
        return dot_nn(left, high[b, j]) + dot_nn(left, low[b, j]) + dot_nn(low[b, i, rows, :], high[b, j])

    def tiles(step):
        @pl.loop(0, K // TILE)
        def _(t):
            start = pl.multiple_of(t * TILE, TILE)
            for b in range(2):
                step(b, pl.ds(start, TILE), start)

    def times(v, b, k):
        parts = split_rows(v)
        return jnp.sum(dot_nn(parts, high[b, k]) + dot_nn(parts, low[b, k]), axis=0, keepdims=True)

    R, F0, R1, M, Q, T, G, Z = range(8)
    inverse = []
    for b in range(2):
        diagonal = jnp.where(
            lax.broadcasted_iota(jnp.int32, (K, K), 0) == lax.broadcasted_iota(jnp.int32, (K, K), 1),
            F32(K - 1.0), F32(0.0))
        system = full[b] + diagonal
        full[b] = system
        sums = jnp.sum(jnp.abs(system), axis=0, keepdims=True)
        inverse.append(1.0 / jnp.max(sums, axis=1, keepdims=True))

    def scaled(b, rows, start):
        value = full[b, rows, :] * inverse[b]
        put(b, R, rows, value)
        put(b, F0, rows, identity_rows(start, 1.5) - 0.5 * value)

    def first(b, rows, start):
        put(b, R1, rows, 1.5 * full[b, rows, :] * inverse[b] - 0.5 * product(b, R, R, rows))

    def second(b, rows, start):
        put(b, M, rows, product(b, F0, R1, rows))

    def third(b, rows, start):
        value = product(b, M, M, rows)
        put(b, Q, rows, value)
        put(b, T, rows, identity_rows(start, 1.6875) - 0.5625 * held(b, M, rows) + 0.0625 * value)

    def fourth(b, rows, start):
        put(b, G, rows, identity_rows(start, 2.25) - 2.4375 * held(b, M, rows) + product(b, Q, T, rows))

    def fifth(b, rows, start):
        value = product(b, G, F0, rows)
        full[b, rows, :] = value
        put(b, Z, rows, value)

    for step in (scaled, first, second, third, fourth, fifth):
        tiles(step)

    mean_weight = [
        times(times(jnp.sum(forcing[b], axis=0, keepdims=True), b, Z), b, Z) * inverse[b] for b in range(2)
    ]
    scale = [jnp.sqrt((K - 1.0) * inverse[b]) for b in range(2)]

    def weights(b, rows, start):
        trans[b, rows, :] = (scale[b] * full[b, rows, :] + mean_weight[b]).astype(BF16)

    tiles(weights)

    for piece in range(PIECES):
        cols = pl.ds(piece * WIDTH, WIDTH)
        drain(arrived.at[:, :, cols], st_recv.at[piece])
        chunk = arrived[:, :, piece * WIDTH : (piece + 1) * WIDTH].astype(F32)
        blocks = []
        for b in range(2):
            values = chunk[:, 8 * b : 8 * b + 8, :].reshape(K, WIDTH)
            mean = jnp.mean(values, axis=0, keepdims=True)
            analysed = mean + dot_nn(trans[b], (values - mean).astype(BF16))
            blocks.append(analysed.reshape(64, 8, WIDTH))
        results[:, :, piece * WIDTH : (piece + 1) * WIDTH] = jnp.concatenate(blocks, axis=1).astype(BF16)

        def give_back(t, carry):
            step = lax.div(t, NX)
            zz = lax.rem(inner + step, 8) + 8 * lax.div(step, 8)
            xx = lax.rem(x + t, NX)
            pass_on(results.at[slot_of(zz, xx), :, cols], out.at[inner * 8 + place, :, cols], out_send, out_recv,
                    device(zz, xx, y, half), (zz == z) & (xx == x) & holder)
            return carry

        lax.fori_loop(0, 64, give_back, 0)

    drain(out, out_recv)

    @pl.when(holder)
    def _():
        drain(meta.at[pl.ds(0, 384)], meta_send)
        drain(chunks.at[pl.ds(0, 63)], st_send)
        drain(results.at[pl.ds(0, 63)], out_send)

    @pl.when(jnp.logical_not(holder))
    def _():
        drain(chunks, st_send)
        drain(results, out_send)

    for q in range(8):
        kept = sum(0 <= q + t - 2 <= 7 for t in range(PAIRS))

        @pl.when(place == q)
        def _():
            drain(own_obs.at[:, pl.ds(0, (8 - kept) * 16)], win_send)

    for _ in range(4):
        drain(own_obs, win_send)


def on_device(states, observed, precision, innovation, column, nearby):
    vmem = pl.BlockSpec(memory_space=pltpu.VMEM)
    dma = pltpu.SemaphoreType.DMA
    gathered = pl.pallas_call(
        kernel,
        out_shape=jax.ShapeDtypeStruct((64, 16, SITES), BF16),
        in_specs=[pl.BlockSpec(memory_space=pltpu.HBM)] * 6,
        out_specs=pl.BlockSpec(memory_space=pltpu.HBM),
        scratch_shapes=[
            pltpu.VMEM((8, 128, SITES), BF16),
            pltpu.VMEM((8, 128, OBS), BF16),
            pltpu.VMEM((128, OBS), F32),
            pltpu.VMEM((128, OBS), F32),
            pltpu.VMEM((128, OBS), jnp.int32),
            pltpu.VMEM((3, 128), jnp.int32),
            dma((6,)),
            pltpu.VMEM((SITES // 128 * 1024, 128), F32),
            pltpu.VMEM((64, 16, SITES), BF16),
            pltpu.VMEM((1024, OBS), BF16),
            pltpu.VMEM((1024, 128), F32),
            pltpu.VMEM((8, 128, OBS), BF16),
            pltpu.VMEM((PAIRS, 64, 16, OBS), BF16),
            pltpu.VMEM((64, 16, SITES), BF16),
            pltpu.VMEM((64, 16, SITES), BF16),
            pltpu.VMEM((256, 128), F32),
            pltpu.VMEM((2, 2, K, OBS), BF16),
            pltpu.VMEM((2, 8, K, K), BF16),
            pltpu.VMEM((2, 8, K, K), BF16),
            pltpu.VMEM((2, K, K), F32),
            pltpu.VMEM((2, K, K), BF16),
            dma, dma, dma, dma, dma, dma((PAIRS,)), dma, dma((PIECES,)), dma, dma, pltpu.SemaphoreType.REGULAR,
        ],
        compiler_params=pltpu.CompilerParams(
            collective_id=0, has_side_effects=True, vmem_limit_bytes=56 * 1024 * 1024
        ),
    )(states, observed, precision, innovation, column, nearby.T)
    return gathered.reshape(64, 2, 8, SITES).transpose(2, 0, 1, 3).reshape(8, 128, SITES)


def solution(mesh):
    split = P("region", None)
    placed = (P("member", "region", None), P("member", "region", None), split, split, split, split)
    return jax.shard_map(
        on_device, mesh=mesh, in_specs=placed, out_specs=P("member", "region", None), check_vma=False
    )
```

time: 197 us -> 182 us (0.924)
  the two profiles are of different devices: /device:TPU:1 before, /device:TPU:24 now
where the time goes in v2:
time: 182 us; the launch traced here: 178 us
  Pallas kernels  175 us (96%)
  local copies, waits for them, and re-layouts  2.84 us (2%)
    pallas_call x1, Pallas kernels, on_device(): pl.pallas_call(kernel, out_shape=jax.ShapeDtypeStruct((64, 16, SITES), BF...  175 us

profile of v2, /device:TPU:24, one launch (start us, length us, event | category | flops | bytes accessed | tf_op | source)
XLA Modules:
  0.0 178.3 jit_solution(2905872722752311102)
XLA Ops:
  0.0 175.4 %shard_map.64 = bf16[64,16,768]{2,1,0:T(8,128)(2,1)} custom-call(bf16[8,128,768]{2,1,0:T(8,128)(2,1)} %states_hbm.1, bf16[8,128,256]{2,1,0:T(8,128)(2,1)} %observed_hbm.1, f32[128,256]{1,0:T(8,128)} %precision_hbm.1, f32[128,256]{1,0:T(8,128)} %innovation_hbm.1, s32[128,256]{1,0:T(8,128)} %column_hbm.1, s32[3,128]{1,0:T(4,128)} %bitcast.7), custom_call_target="tpu_custom_call" | custom-call | tf_op jit(solution)/shard_map/pallas_call | solution.py:376
  175.4 2.8 %copy.8 = bf16[8,128,768]{2,1,0:T(8,128)(2,1)} copy(bf16[8,128,768]{2,0,1:T(8,128)(2,1)} %bitcast.6) | data formatting | bytes 3145728 | tf_op jit(solution)/shard_map/reshape | solution.py:409

commit v3 on v2

--- a/solution.py
+++ b/solution.py
@@ -127,8 +127,6 @@
     by_block(observed, obs)
     pl.semaphore_wait(barrier, 39 - 2 * self_obs.astype(jnp.int32))
 
-    for j in range(8):
-        greet(row_ready, 2 * j + c, x, y, half)
 
     def send_obs(t, carry):
         ii = lax.rem(inner + t, 8)
@@ -139,6 +137,9 @@
         return carry
 
     lax.fori_loop(0, 8, send_obs, 0)
+
+    for j in range(8):
+        greet(row_ready, 2 * j + c, x, y, half)
 
     loads[1].wait()
     by_block(states, chunks)
@@ -377,7 +378,7 @@
         kernel,
         out_shape=jax.ShapeDtypeStruct((64, 16, SITES), BF16),
         in_specs=[pl.BlockSpec(memory_space=pltpu.HBM)] * 6,
-        out_specs=pl.BlockSpec(memory_space=pltpu.HBM),
+        out_specs=vmem,
         scratch_shapes=[
             pltpu.VMEM((8, 128, SITES), BF16),
             pltpu.VMEM((8, 128, OBS), BF16),
@@ -403,9 +404,10 @@
             dma, dma, dma, dma, dma, dma((PAIRS,)), dma, dma((PIECES,)), dma, dma, pltpu.SemaphoreType.REGULAR,
         ],
         compiler_params=pltpu.CompilerParams(
-            collective_id=0, has_side_effects=True, vmem_limit_bytes=56 * 1024 * 1024
+            collective_id=0, has_side_effects=True, vmem_limit_bytes=44 * 1024 * 1024
         ),
-    )(states, observed, precision, innovation, column, nearby.T)
+    )(*(pltpu.with_memory_space_constraint(a, pltpu.HBM)
+        for a in (states, observed, precision, innovation, column, nearby.T)))
     return gathered.reshape(64, 2, 8, SITES).transpose(2, 0, 1, 3).reshape(8, 128, SITES)
 
 

time: 182 us -> 180 us (0.989)
  no operation moved by 1% of the time
where the time goes in v3:
time: 180 us; the launch traced here: 177 us
  Pallas kernels  176 us (98%)
    pallas_call x1, Pallas kernels, on_device(): pl.pallas_call(kernel, out_shape=jax.ShapeDtypeStruct((64, 16, SITES), BF...  176 us

profile of v3, /device:TPU:24, one launch (start us, length us, event | category | flops | bytes accessed | tf_op | source)
XLA Modules:
  0.0 177.2 jit_solution(13911046755679993073)
XLA Ops:
  0.0 175.7 %shard_map.64 = bf16[64,16,768]{2,1,0:T(8,128)(2,1)S(1)} custom-call(bf16[8,128,768]{2,1,0:T(8,128)(2,1)} %states_hbm.1, bf16[8,128,256]{2,1,0:T(8,128)(2,1)} %observed_hbm.1, f32[128,256]{1,0:T(8,128)} %precision_hbm.1, f32[128,256]{1,0:T(8,128)} %innovation_hbm.1, s32[128,256]{1,0:T(8,128)} %column_hbm.1, s32[3,128]{1,0:T(4,128)} %bitcast.7), custom_call_target="tpu_custom_call" | custom-call | tf_op jit(solution)/shard_map/pallas_call | solution.py:377
  175.8 1.4 copy.8

commit v4 on v3

--- a/solution.py
+++ b/solution.py
@@ -55,7 +55,7 @@
     states, observed, precision, innovation, column, nearby, load_sem,
     wide, chunks, obs, meta, own_obs, window, arrived, results, meta_win, weighted, high, low, full, trans,
     meta_send, meta_recv, obs_send, obs_recv, win_send, win_recv, st_send, st_recv, out_send, out_recv,
-    row_ready,
+    row_ready, end_send,
 ):
     member = lax.axis_index("member")
     region = lax.axis_index("region")
@@ -205,6 +205,8 @@
     mine_at = pl.ds(pl.multiple_of(place * 8, 8), 8)
     for t in range(PAIRS):
 
+        skipped = {0: 7, PAIRS - 1: 0}.get(t, -1)
+
         def send_pair(step, carry):
             u = lax.rem(place + step, 8)
             q = u + 2 - t
@@ -214,8 +216,12 @@
                 lax.select(q < 0, y_prev, lax.select(q > 7, y_next, y)),
                 lax.rem(q + 8, 2),
             )
-            pass_on(own_obs.at[:, pl.ds(pl.multiple_of(u * 16, 16), 16)], window.at[t, mine_at],
-                    win_send, win_recv.at[t], target, q == place)
+
+            @pl.when(u != skipped)
+            def _():
+                pass_on(own_obs.at[:, pl.ds(pl.multiple_of(u * 16, 16), 16)], window.at[t, mine_at],
+                        win_send, win_recv.at[t], target, q == place)
+
             return carry
 
         lax.fori_loop(0, 8, send_pair, 0)
@@ -229,8 +235,20 @@
 
     listed_by = [meta_of(8 + 2 * place + b)[6:7] for b in range(2)]
     forcing = [jnp.zeros((16, K), F32) for _ in range(2)]
+    for end, came, goes in ((0, 1, 0), (7, 3, 4)):
+
+        @pl.when(place == end)
+        def _():
+            drain(window.at[came], win_recv.at[came])
+            remote(window.at[came], window.at[goes], end_send, win_recv.at[goes], device(z, x, y, 1 - c))
+
     for t in range(PAIRS):
-        drain(window.at[t], win_recv.at[t])
+        taken = ((place == 0) & (t == 1)) | ((place == 7) & (t == 3))
+
+        @pl.when(jnp.logical_not(taken))
+        def _():
+            drain(window.at[t], win_recv.at[t])
+
         rows = window[t].astype(F32)
         perts, innov = [], []
         for e in range(2):
@@ -360,12 +378,16 @@
         drain(chunks, st_send)
         drain(results, out_send)
 
+    @pl.when((place == 0) | (place == 7))
+    def _():
+        drain(window.at[0], end_send)
+
     for q in range(8):
         kept = sum(0 <= q + t - 2 <= 7 for t in range(PAIRS))
 
         @pl.when(place == q)
         def _():
-            drain(own_obs.at[:, pl.ds(0, (8 - kept) * 16)], win_send)
+            drain(own_obs.at[:, pl.ds(0, (6 - kept) * 16)], win_send)
 
     for _ in range(4):
         drain(own_obs, win_send)
@@ -401,7 +423,7 @@
             pltpu.VMEM((2, 8, K, K), BF16),
             pltpu.VMEM((2, K, K), F32),
             pltpu.VMEM((2, K, K), BF16),
-            dma, dma, dma, dma, dma, dma((PAIRS,)), dma, dma((PIECES,)), dma, dma, pltpu.SemaphoreType.REGULAR,
+            dma, dma, dma, dma, dma, dma((PAIRS,)), dma, dma((PIECES,)), dma, dma, pltpu.SemaphoreType.REGULAR, dma,
         ],
         compiler_params=pltpu.CompilerParams(
             collective_id=0, has_side_effects=True, vmem_limit_bytes=44 * 1024 * 1024

time: 180 us -> 179 us (level)
  Pallas kernels: 176 us -> 174 us
where the time goes in v4:
time: 179 us; the launch traced here: 175 us
  Pallas kernels  174 us (97%)
    pallas_call x1, Pallas kernels, on_device(): pl.pallas_call(kernel, out_shape=jax.ShapeDtypeStruct((64, 16, SITES), BF...  174 us

profile of v4, /device:TPU:24, one launch (start us, length us, event | category | flops | bytes accessed | tf_op | source)
XLA Modules:
  0.0 175.4 jit_solution(13524427680876082737)
XLA Ops:
  0.0 174.0 %shard_map.64 = bf16[64,16,768]{2,1,0:T(8,128)(2,1)S(1)} custom-call(bf16[8,128,768]{2,1,0:T(8,128)(2,1)} %states_hbm.1, bf16[8,128,256]{2,1,0:T(8,128)(2,1)} %observed_hbm.1, f32[128,256]{1,0:T(8,128)} %precision_hbm.1, f32[128,256]{1,0:T(8,128)} %innovation_hbm.1, s32[128,256]{1,0:T(8,128)} %column_hbm.1, s32[3,128]{1,0:T(4,128)} %bitcast.7), custom_call_target="tpu_custom_call" | custom-call | tf_op jit(solution)/shard_map/pallas_call | solution.py:399
  174.0 1.4 copy.8
